TPU v7x, 512 devices: a whole 4x4x16 slice. The times are simulated.
512 devices in a mesh: seq: 32 (over z, y_lo), mp: 16 (over x, y_hi, core).
Axes of the slice: x: 4, y: 4 (y_hi: 2, y_lo: 2; y = y_hi * 2 + y_lo), z: 16, core: 2. Of those that a mesh axis runs over, the one named last changes fastest.
Arguments:
- queries: bfloat16 [16384, 8192], P('seq', 'mp'), may hold values from -6 to 6
- keys_in: bfloat16 [16384, 8192], P('seq', 'mp'), may hold values from -6 to 6
- values_in: bfloat16 [16384, 8192], P('seq', 'mp'), may hold values from -6 to 6
- residual: bfloat16 [16384, 8192], P('seq', 'mp')
- short_taps: bfloat16 [3, 7, 8192], P(None, None, 'mp'), may hold values from -2 to 2
- mr_filter: bfloat16 [128, 512], P('seq', 'mp'), may hold values from -0.5 to 0.5
- norm_gain: bfloat16 [8192], P('mp'), may hold values from 0.5 to 1.5
- predecessor: int32 [32], replicated, may hold values from -1 to 31, as said below
- stretch_lengths: int32 [32], replicated, may hold values from 1 to 512, as said below
Outputs:
- mixed: bfloat16 [16384, 8192], P('seq', 'mp')
- normed: bfloat16 [16384, 8192], P('seq', 'mp')
Inputs may be any that keep to these rules, and one draw needn't show every extreme that they name: predecessor[j] is the stretch holding the preceding 512 tokens of stretch j's genome, or -1 for a genome's first stretch; each stretch precedes at most one stretch, and the chains have no cycles. `stretch_lengths`: every stretch that precedes another stretch is full (512 valid tokens); valid tokens come first.
All inputs are finite; a program needn't handle non-finite values.
Results may differ from a plain program's by a relative error of at most 0.0049.
Values may be sent and summed in bfloat16 or wider, within the bound.
A program may use at most 64 MiB of HBM per device.

v0:
```python
import jax
import jax.numpy as jnp
from jax import lax
from jax.sharding import PartitionSpec as P

EPSILON = 1e-06


def featurize(extended, taps):
    length = extended.shape[0] - 8
    total = jnp.zeros((length, extended.shape[1]), jnp.float32)
    for offset in range(taps.shape[0]):
        total = total + taps[offset].astype(jnp.float32) * extended[
            8 - offset : 8 - offset + length
        ].astype(jnp.float32)
    return total


def toeplitz_blocks(filter_rows):
    tap_count = filter_rows.shape[0]
    group_count = filter_rows.shape[1]
    flipped = filter_rows[::-1].T
    pattern = jnp.concatenate(
        [
            jnp.zeros((group_count, 1), filter_rows.dtype),
            flipped,
            jnp.zeros((group_count, tap_count), filter_rows.dtype),
        ],
        axis=1,
    )
    tiled = jnp.tile(pattern, (1, tap_count))[:, : 2 * tap_count * tap_count]
    return tiled.reshape(group_count, tap_count, 2 * tap_count)


def long_conv(extended, filter_rows, group_size):
    tap_count = filter_rows.shape[0]
    length = extended.shape[0] - tap_count
    blocks = length // tap_count
    channels = extended.shape[1]
    pieces = extended.reshape(blocks + 1, tap_count, channels)
    windows = jnp.concatenate([pieces[:-1], pieces[1:]], axis=1).reshape(
        blocks, 2 * tap_count, channels // group_size, group_size
    )
    matrices = toeplitz_blocks(filter_rows)
    result = jnp.einsum("gij,bjgc->bigc", matrices, windows, preferred_element_type=jnp.float32)
    return result.reshape(length, channels)


def body(
    queries,
    keys_in,
    values_in,
    residual,
    short_taps,
    mr_filter,
    norm_gain,
    predecessor,
    stretch_lengths,
):
    row_count, width = queries.shape
    device = lax.axis_index("seq")
    filter_rows = lax.all_gather(mr_filter, "seq", axis=0, tiled=True)
    tap_count = filter_rows.shape[0]
    group_size = width // filter_rows.shape[1]
    blank = jnp.zeros((8, width), queries.dtype)
    key_feat = featurize(jnp.concatenate([blank, keys_in]), short_taps[1])
    value_feat = featurize(jnp.concatenate([blank, values_in]), short_taps[2])
    mixed_in = (key_feat * value_feat).astype(jnp.bfloat16)
    state_tail = mixed_in[row_count - tap_count :][None]
    raw_tail = jnp.concatenate(
        [queries[row_count - 8 :], keys_in[row_count - 8 :], values_in[row_count - 8 :]], axis=1
    )[None]
    source = predecessor[device]
    carry = (jnp.zeros_like(state_tail), jnp.zeros_like(raw_tail))
    piece = (
        lax.all_gather(state_tail, "seq", axis=0, tiled=True),
        lax.all_gather(raw_tail, "seq", axis=0, tiled=True),
    )
    count = piece[0].shape[0]
    inside = (source >= 0) & (source < count)
    offset = jnp.clip(source, 0, count - 1)
    prev_state, prev_raw = tuple(
        (
            jnp.where(inside, lax.dynamic_slice_in_dim(member, offset, 1, 0), kept)
            for member, kept in zip(piece, carry)
        )
    )
    prev_rows = prev_raw[0]
    prev_query = prev_rows[:, :width]
    prev_key = prev_rows[:, width : 2 * width]
    prev_value = prev_rows[:, 2 * width :]
    query_feat = featurize(jnp.concatenate([prev_query, queries]), short_taps[0])
    head_key = featurize(jnp.concatenate([prev_key, keys_in[:8]]), short_taps[1])
    head_value = featurize(jnp.concatenate([prev_value, values_in[:8]]), short_taps[2])
    head_mixed = (head_key * head_value).astype(jnp.bfloat16)
    mixed_in = jnp.concatenate([head_mixed, mixed_in[8:]])
    extended = jnp.concatenate([prev_state[0], mixed_in])
    filtered = long_conv(extended, filter_rows, group_size)
    valid = (jnp.arange(row_count, dtype=jnp.int32) < stretch_lengths[device])[:, None]
    mixed = jnp.where(valid, query_feat * filtered, 0.0).astype(jnp.bfloat16)
    summed = residual.astype(jnp.float32) + mixed.astype(jnp.float32)
    squares_total = lax.psum(jnp.sum(summed * summed, axis=1), "mp")
    scale_rows = lax.rsqrt(squares_total / (width * lax.axis_size("mp")) + EPSILON)
    normed = jnp.where(
        valid, summed * scale_rows[:, None] * norm_gain.astype(jnp.float32), 0.0
    ).astype(jnp.bfloat16)
    return (mixed, normed)


def solution(mesh):
    in_specs = (
        P("seq", "mp"),
        P("seq", "mp"),
        P("seq", "mp"),
        P("seq", "mp"),
        P(None, None, "mp"),
        P("seq", "mp"),
        P("mp"),
        P(),
        P(),
    )
    out_specs = (P("seq", "mp"), P("seq", "mp"))
    return jax.shard_map(body, mesh=mesh, in_specs=in_specs, out_specs=out_specs, check_vma=False)
```

profile of v0, /device:TPU:1, one launch (start us, length us, event | category | flops | bytes accessed | tf_op | source)
XLA Modules:
  0.0 226.0 jit_solution(18346637916515088260)
XLA Ops:
  7.2 0.0 copy-start.3
  7.2 0.0 all-gather.5.cloned.1.call-start
  7.2 1.0 slice_convert_fusion.20
  8.2 0.0 copy-start.4
  8.2 0.8 slice_convert_fusion.1
  9.0 5.3 %multiply_convert_fusion = bf16[512,512]{1,0:T(8,128)(2,1)S(1)} fusion(bf16[512,512]{1,0:T(8,128)(2,1)} %param.11, bf16[512,512]{1,0:T(8,128)(2,1)} %param.10, f32[512]{0:T(512)S(1)} %bitcast.92, f32[512]{0:T(512)S(1)} %bitcast.90, f32[512]{0:T(512)S(1)} %bitcast.66, f32[512]{0:T(512)S(1)} %bitcast.68, f32[512]{0:T(512)S(1)} %bitcast.70, ...), kind=kLoop, calls=%fused_computation.17 | loop fusion | flops 11010048 | bytes 1601536 | tf_op jit(solution)/shard_map/convert_element_type | solution.py:68
  14.4 0.0 copy-start
  14.4 0.7 slice.328
  15.1 0.0 all-gather.5.cloned.1.call-update
  15.2 0.6 dynamic_slice.13
  16.9 1.0 copy.66
  18.5 0.0 copy-done.4
  18.5 56.7 %all-gather.2 = bf16[32,4,32]{2,1,0:T(4,128)(2,1)S(1)} all-gather(bf16[1,4,32]{2,1,0:T(4,128)(2,1)S(1)} %bitcast.102), channel_id=1, replica_groups=mesh['seq'=32,'mp'=16] {'seq'}, dimensions={0}, use_global_device_ids=true | all-gather | bytes 8448 | tf_op jit(solution)/shard_map/all_gather | solution.py:62
  75.2 0.1 copy.73
  75.3 0.1 rev.3
  75.4 0.1 pad.4.clone
  75.5 0.1 maximum_maximum_fusion
  75.6 0.3 tile.4
  75.8 4.4 %tile.10 = bf16[32,32896]{1,0:T(8,128)(2,1)} reshape(bf16[32,128,257]{2,1,0:T(8,128)(2,1)S(1)} %tile.4) | data formatting | bytes 4210688 | tf_op jit(solution)/shard_map/tile | solution.py:31
  80.3 1.6 slice-done
  81.9 0.5 copy.79
  82.4 0.0 copy-start.5
  82.4 0.0 slice-start.1
  82.4 0.8 fusion.27
  83.2 59.5 %all-gather = bf16[256,1536]{1,0:T(8,128)(2,1)S(1)} all-gather(bf16[8,1536]{1,0:T(8,128)(2,1)S(1)} %pad_maximum_fusion.4), channel_id=2, replica_groups=mesh['seq'=32,'mp'=16] {'seq'}, dimensions={0}, use_global_device_ids=true | all-gather | bytes 811008 | tf_op jit(solution)/shard_map/all_gather | solution.py:77
  142.8 0.2 copy.67
  143.0 0.0 copy-done.7
  143.0 0.7 dynamic_slice.12
  143.6 1.3 copy.75
  144.9 0.7 iota_compare_fusion
  145.6 0.1 multiply_convert_fusion.1
  145.7 4.9 %all-gather.5.cloned.1.call-done = bf16[4096,512]{1,0:T(8,128)(2,1)} async-done(((bf16[128,512]{1,0:T(8,128)(2,1)}), bf16[4096,512]{1,0:T(8,128)(2,1)}) %all-gather.5.cloned.1.call-update) | async-done | bytes 4194320 | tf_op jit(solution)/shard_map/all_gather | solution.py:76
  150.6 0.9 select_bitcast_fusion
  151.5 1.0 pad_maximum_fusion
  152.6 2.1 copy.69
  154.7 2.0 concatenate.42
  156.7 1.9 copy.71
  158.6 1.0 copy.70
  159.6 1.2 concatenate.44
  160.8 0.1 copy.72
  160.9 1.9 fusion.2
  162.8 0.4 copy.74
  163.2 0.6 copy-done.2
  163.8 2.1 multiply_reduce_fusion
  165.9 51.0 %psum.7 = f32[512]{0:T(512)S(1)} all-reduce(f32[512]{0:T(512)S(1)} %get-tuple-element.8), channel_id=1, replica_groups=mesh['seq'=32,'mp'=16] {'mp'}, use_global_device_ids=true, to_apply=%region_1.2 | all-reduce | flops 512 | bytes 4096 | tf_op jit(solution)/shard_map/psum | solution.py:102
  216.9 1.0 copy.76
  217.9 0.2 select_convert_fusion
  218.1 1.0 copy.77
  (20 shorter events, 0.1 us)
Async XLA Ops:
  7.2 8.0 %copy-start.6 = (s32[32]{0:T(128)S(1)}, s32[32]{0:T(128)}, u32[]{:S(2)}) copy-start(s32[32]{0:T(128)} %param.16) | copy-start | bytes 388
  7.2 9.7 %copy-start.3 = (bf16[512,512]{1,0:T(8,128)(2,1)S(1)}, bf16[512,512]{1,0:T(8,128)(2,1)}, u32[]{:S(2)}) copy-start(bf16[512,512]{1,0:T(8,128)(2,1)} %param.9) | copy-start | bytes 1572868
  7.2 143.4 %all-gather.5.cloned.1.call-start = ((), (), s32[]{:S(2)}) async-start(), calls=%async_computation | async-start | bytes 4325376 | tf_op jit(solution)/shard_map/all_gather | solution.py:76
  8.2 10.2 %copy-start.4 = (bf16[4,32]{1,0:T(4,128)(2,1)S(1)}, bf16[4,32]{1,0:T(4,128)(2,1)}, u32[]{:S(2)}) copy-start(bf16[4,32]{1,0:T(4,128)(2,1)} %param.14) | copy-start | bytes 772
  14.4 61.1 %copy-start = (bf16[512,512]{1,0:T(8,128)(2,1)}, bf16[512,512]{1,0:T(8,128)(2,1)S(1)}, u32[]{:S(2)}) copy-start(bf16[512,512]{1,0:T(8,128)(2,1)S(1)} %multiply_convert_fusion) | copy-start | bytes 1572868
  80.3 1.6 slice-start
  81.9 1.3 slice-start.2
  81.9 61.1 %copy-start.7 = (s32[32]{0:T(128)S(1)}, s32[32]{0:T(128)}, u32[]{:S(2)}) copy-start(s32[32]{0:T(128)} %param.17) | copy-start | bytes 388
  82.4 62.5 %copy-start.5 = (bf16[512]{0:T(512)(128)(2,1)S(1)}, bf16[512]{0:T(512)(128)(2,1)}, u32[]{:S(2)}) copy-start(bf16[512]{0:T(512)(128)(2,1)} %param.15) | copy-start | bytes 3076
  82.4 69.1 %slice-start.1 = ((bf16[512,512]{1,0:T(8,128)(2,1)}), bf16[504,512]{1,0:T(8,128)(2,1)S(1)}, s32[]{:S(2)}) async-start(bf16[512,512]{1,0:T(8,128)(2,1)} %copy-done), calls=%async_computation.2 | async-start | bytes 1032192 | tf_op jit(solution)/shard_map/slice | solution.py:96
  152.6 6.0 %copy-start.1 = (bf16[512,512]{1,0:T(8,128)(2,1)S(1)}, bf16[512,512]{1,0:T(8,128)(2,1)}, u32[]{:S(2)}) copy-start(bf16[512,512]{1,0:T(8,128)(2,1)} %get-tuple-element.11) | copy-start | bytes 1572868
  162.8 1.0 copy-start.2
Sparse Core Ops, SparseCore 0:
  15.3 135.2 all-gather.4
where the time goes:
time: 227 us; the launch traced here: 226 us
  blocking collectives  167 us (74%)
  local copies, waits for them, and re-layouts  23.7 us (10%)
  between operations  16 us (7%)
  other arithmetic  12.3 us (5%)
  waiting for transfers between devices  4.95 us (2%)
    all_gather x1, blocking collectives, body(): lax.all_gather(raw_tail, 'seq', axis=0, tiled=True)  59.5 us
    all_gather x1, blocking collectives, body(): filter_rows = lax.all_gather(mr_filter, 'seq', axis=0, tiled=True)  56.7 us
    psum x1, blocking collectives, body(): squares_total = lax.psum(jnp.sum(summed * summed, axis=1), 'mp')  51 us
    unnamed x22, local copies, waits for them, and re-layouts  5.46 us
    convert_element_type x1, other arithmetic, body(): mixed_in = (key_feat * value_feat).astype(jnp.bfloat16)  5.34 us
    concatenate x4, local copies, waits for them, and re-layouts, long_conv(): jnp.concatenate([pieces[:-1], pieces[1:]], axis=1)  5.16 us
    all_gather x1, waiting for transfers between devices, body(): lax.all_gather(state_tail, 'seq', axis=0, tiled=True)  4.93 us
    another operation x2, local copies, waits for them, and re-layouts, toeplitz_blocks(): tiled = jnp.tile(pattern, (1, tap_count))[:, :2 * tap_count * tap_count]  4.73 us
  transfers between devices with their start and end apart: 1, of which 1 were waited for; matrix products, arithmetic and copies ran while one was open for 5% of the time, Pallas kernels for 0%

commit v1 on v0

--- a/solution.py
+++ b/solution.py
@@ -4,6 +4,11 @@
 from jax.sharding import PartitionSpec as P
 
 EPSILON = 1e-06
+
+
+def exchange_gather(array, mesh_axis, d):
+    stack = jnp.stack([array] * lax.axis_size(mesh_axis))
+    return jnp.concatenate(lax.all_to_all(stack, mesh_axis, 0, 0), axis=d)
 
 
 def featurize(extended, taps):
@@ -74,7 +79,7 @@
     carry = (jnp.zeros_like(state_tail), jnp.zeros_like(raw_tail))
     piece = (
         lax.all_gather(state_tail, "seq", axis=0, tiled=True),
-        lax.all_gather(raw_tail, "seq", axis=0, tiled=True),
+        exchange_gather(raw_tail, "seq", 0),
     )
     count = piece[0].shape[0]
     inside = (source >= 0) & (source < count)

time: 227 us -> 238 us (1.048)
  blocking collectives: 167 us -> 131 us
  waiting for transfers between devices: 4.95 us -> 28.7 us
  starting transfers between devices: 0.04 us -> 17.2 us
  local copies, waits for them, and re-layouts: 23.7 us -> 26.3 us
  other arithmetic: 12.3 us -> 14.8 us
    all_gather x1 -> x0, blocking collectives: 59.5 us -> none  [body(): lax.all_gather(raw_tail, 'seq', axis=0, tiled=True)]
    all_gather x1, blocking collectives: 56.7 us -> 81.8 us  [body(): filter_rows = lax.all_gather(mr_filter, 'seq', axis=0, tiled=True)]
    all_gather x1, waiting for transfers between devices: 4.93 us -> 28.7 us  [body(): lax.all_gather(state_tail, 'seq', axis=0, tiled=True)]
    all_to_all x0 -> x1, starting transfers between devices: none -> 17.2 us  [exchange_gather(): return jnp.concatenate(lax.all_to_all(stack, mesh_axis, 0, 0), axis=d)]
    unnamed x22 -> x69, local copies, waits for them, and re-layouts: 5.46 us -> 5.89 us
  transfers between devices with their start and end apart: 1 -> 2, of which waited for: 1 -> 1; matrix products, arithmetic and copies ran while one was open for 5% -> 7% of each run, Pallas kernels for 0% -> 0%
where the time goes in v1:
time: 238 us; the launch traced here: 237 us
  blocking collectives  131 us (55%)
  waiting for transfers between devices  28.7 us (12%)
  local copies, waits for them, and re-layouts  26.3 us (11%)
  starting transfers between devices  17.2 us (7%)
  between operations  16.6 us (7%)
  other arithmetic  14.8 us (6%)
    all_gather x1, blocking collectives, body(): filter_rows = lax.all_gather(mr_filter, 'seq', axis=0, tiled=True)  81.8 us
    psum x1, blocking collectives, body(): squares_total = lax.psum(jnp.sum(summed * summed, axis=1), 'mp')  49.5 us
    all_gather x1, waiting for transfers between devices, body(): lax.all_gather(state_tail, 'seq', axis=0, tiled=True)  28.7 us
    all_to_all x1, starting transfers between devices, exchange_gather(): return jnp.concatenate(lax.all_to_all(stack, mesh_axis, 0, 0), axis=d)  17.2 us
    unnamed x69, local copies, waits for them, and re-layouts  5.89 us
    convert_element_type x1, other arithmetic, body(): mixed_in = (key_feat * value_feat).astype(jnp.bfloat16)  5.19 us
    concatenate x4, local copies, waits for them, and re-layouts, long_conv(): jnp.concatenate([pieces[:-1], pieces[1:]], axis=1)  5.13 us
  transfers between devices with their start and end apart: 2, of which 1 were waited for; matrix products, arithmetic and copies ran while one was open for 7% of the time, Pallas kernels for 0%

profile of v1, /device:TPU:1, one launch (start us, length us, event | category | flops | bytes accessed | tf_op | source)
XLA Modules:
  0.0 236.7 jit_solution(613467459014642783)
XLA Ops:
  7.2 0.0 slice-start.2
  7.2 0.0 all-gather.4.cloned.1.call-start
  7.2 1.6 slice_convert_fusion.20
  8.9 0.8 slice_convert_fusion.1
  9.7 5.2 %multiply_convert_fusion = bf16[512,512]{1,0:T(8,128)(2,1)S(1)} fusion(bf16[512,512]{1,0:T(8,128)(2,1)} %param.11, bf16[512,512]{1,0:T(8,128)(2,1)} %param.10, f32[512]{0:T(512)S(1)} %bitcast.90, f32[512]{0:T(512)S(1)} %bitcast.88, f32[512]{0:T(512)S(1)} %bitcast.64, f32[512]{0:T(512)S(1)} %bitcast.66, f32[512]{0:T(512)S(1)} %bitcast.68, ...), kind=kLoop, calls=%fused_computation.17 | loop fusion | flops 11010048 | bytes 1601536 | tf_op jit(solution)/shard_map/convert_element_type | solution.py:73
  15.1 0.7 slice.328
  15.8 0.0 all-gather.4.cloned.1.call-update
  15.8 1.4 fusion.27
  17.2 1.0 stack.3
  18.1 17.2 %all-to-all-start = ((bf16[32,1,8,1536]{3,2,1,0:T(8,128)(2,1)}), bf16[32,1,8,1536]{3,2,1,0:T(8,128)(2,1)}, u32[]{:S(2)}, u32[]{:S(2)}) async-start(bf16[32,1,8,1536]{3,2,1,0:T(8,128)(2,1)} %stack.3), calls=%async_computation | async-start | bytes 1572864 | tf_op jit(solution)/shard_map/all_to_all | solution.py:11
  35.3 0.6 dynamic_slice.13
  37.3 1.0 copy.55
  39.0 81.8 %all-gather.1 = bf16[32,4,32]{2,1,0:T(4,128)(2,1)S(1)} all-gather(bf16[1,4,32]{2,1,0:T(4,128)(2,1)S(1)} %bitcast.100), channel_id=1, replica_groups=mesh['seq'=32,'mp'=16] {'seq'}, dimensions={0}, use_global_device_ids=true | all-gather | bytes 8448 | tf_op jit(solution)/shard_map/all_gather | solution.py:67
  120.9 0.1 copy.64
  120.9 0.1 rev.3
  121.0 0.1 pad.4.clone
  121.1 0.1 maximum_maximum_fusion
  121.2 0.3 tile.4
  121.5 4.5 %tile.10 = bf16[32,32896]{1,0:T(8,128)(2,1)} reshape(bf16[32,128,257]{2,1,0:T(8,128)(2,1)S(1)} %tile.4) | data formatting | bytes 4210688 | tf_op jit(solution)/shard_map/tile | solution.py:36
  126.0 1.6 slice-done
  127.6 0.5 copy.71
  128.1 0.2 copy-done.30
  128.2 0.6 dynamic_slice.12
  128.9 1.3 copy.66
  130.2 0.6 convert_element_type.432
  130.7 1.1 iota_compare_fusion
  131.9 0.7 constant_dynamic-slice_fusion
  132.6 0.2 copy.70
  132.9 0.1 copy.58
  133.0 0.1 copy.59
  133.1 1.1 multiply_convert_fusion.1
  134.2 28.7 %all-gather.4.cloned.1.call-done = bf16[4096,512]{1,0:T(8,128)(2,1)} async-done(((bf16[128,512]{1,0:T(8,128)(2,1)}), bf16[4096,512]{1,0:T(8,128)(2,1)}) %all-gather.4.cloned.1.call-update) | async-done | bytes 4194320 | tf_op jit(solution)/shard_map/all_gather | solution.py:81
  162.8 0.9 select_bitcast_fusion.1
  163.8 1.0 pad_maximum_fusion
  164.8 2.1 copy.60
  166.9 2.0 concatenate.42
  168.9 1.9 copy.62
  170.8 1.0 copy.61
  171.8 1.2 concatenate.44
  173.0 0.1 copy.63
  173.1 1.9 fusion.2
  175.0 0.4 copy.65
  175.5 0.5 copy-done.2
  176.1 2.1 multiply_reduce_fusion
  178.2 49.5 %psum.7 = f32[512]{0:T(512)S(1)} all-reduce(f32[512]{0:T(512)S(1)} %get-tuple-element.6), channel_id=1, replica_groups=mesh['seq'=32,'mp'=16] {'mp'}, use_global_device_ids=true, to_apply=%region_1.2 | all-reduce | flops 512 | bytes 4096 | tf_op jit(solution)/shard_map/psum | solution.py:107
  227.6 1.0 copy.67
  228.6 0.2 select_convert_fusion
  228.9 1.0 copy.68
  (71 shorter events, 0.2 us)
Async XLA Ops:
  7.2 10.0 %slice-start.2 = ((bf16[512,512]{1,0:T(8,128)(2,1)}), bf16[8,512]{1,0:T(8,128)(2,1)S(1)}, s32[]{:S(2)}) async-start(bf16[512,512]{1,0:T(8,128)(2,1)} %param.9), calls=%async_computation.4 | async-start | bytes 16384 | tf_op jit(solution)/shard_map/slice | solution.py:76
  7.2 155.6 %all-gather.4.cloned.1.call-start = ((), (), s32[]{:S(2)}) async-start(), calls=%async_computation.1 | async-start | bytes 4325376 | tf_op jit(solution)/shard_map/all_gather | solution.py:81
  8.8 0.9 copy-start.4
  8.8 6.1 %copy-start.5 = (f32[1,1,512]{2,1,0:T(1,128)}, f32[1,1,512]{2,1,0:T(1,128)S(1)}, u32[]{:S(2)}) copy-start(f32[1,1,512]{2,1,0:T(1,128)S(1)} %get-tuple-element.19) | copy-start | bytes 6148
  8.8 6.1 %copy-start.6 = (f32[1,1,512]{2,1,0:T(1,128)}, f32[1,1,512]{2,1,0:T(1,128)S(1)}, u32[]{:S(2)}) copy-start(f32[1,1,512]{2,1,0:T(1,128)S(1)} %get-tuple-element.20) | copy-start | bytes 6148
  8.8 6.1 %copy-start.7 = (f32[1,1,512]{2,1,0:T(1,128)}, f32[1,1,512]{2,1,0:T(1,128)S(1)}, u32[]{:S(2)}) copy-start(f32[1,1,512]{2,1,0:T(1,128)S(1)} %get-tuple-element.21) | copy-start | bytes 6148
  8.8 6.1 %copy-start.8 = (f32[1,1,512]{2,1,0:T(1,128)}, f32[1,1,512]{2,1,0:T(1,128)S(1)}, u32[]{:S(2)}) copy-start(f32[1,1,512]{2,1,0:T(1,128)S(1)} %get-tuple-element.22) | copy-start | bytes 6148
  8.9 6.1 %copy-start.9 = (f32[1,1,512]{2,1,0:T(1,128)}, f32[1,1,512]{2,1,0:T(1,128)S(1)}, u32[]{:S(2)}) copy-start(f32[1,1,512]{2,1,0:T(1,128)S(1)} %get-tuple-element.23) | copy-start | bytes 6148
  8.9 6.1 %copy-start.10 = (f32[1,1,512]{2,1,0:T(1,128)}, f32[1,1,512]{2,1,0:T(1,128)S(1)}, u32[]{:S(2)}) copy-start(f32[1,1,512]{2,1,0:T(1,128)S(1)} %get-tuple-element.24) | copy-start | bytes 6148
  8.9 6.1 %copy-start.11 = (f32[1,1,512]{2,1,0:T(1,128)}, f32[1,1,512]{2,1,0:T(1,128)S(1)}, u32[]{:S(2)}) copy-start(f32[1,1,512]{2,1,0:T(1,128)S(1)} %get-tuple-element.25) | copy-start | bytes 6148
  8.9 6.1 %copy-start.12 = (f32[1,1,512]{2,1,0:T(1,128)}, f32[1,1,512]{2,1,0:T(1,128)S(1)}, u32[]{:S(2)}) copy-start(f32[1,1,512]{2,1,0:T(1,128)S(1)} %get-tuple-element.26) | copy-start | bytes 6148
  8.9 6.1 %copy-start.13 = (f32[1,1,512]{2,1,0:T(1,128)}, f32[1,1,512]{2,1,0:T(1,128)S(1)}, u32[]{:S(2)}) copy-start(f32[1,1,512]{2,1,0:T(1,128)S(1)} %get-tuple-element.27) | copy-start | bytes 6148
  8.9 6.1 %copy-start.14 = (f32[1,1,512]{2,1,0:T(1,128)}, f32[1,1,512]{2,1,0:T(1,128)S(1)}, u32[]{:S(2)}) copy-start(f32[1,1,512]{2,1,0:T(1,128)S(1)} %get-tuple-element.28) | copy-start | bytes 6148
  8.9 6.1 %copy-start.15 = (f32[1,1,512]{2,1,0:T(1,128)}, f32[1,1,512]{2,1,0:T(1,128)S(1)}, u32[]{:S(2)}) copy-start(f32[1,1,512]{2,1,0:T(1,128)S(1)} %get-tuple-element.29) | copy-start | bytes 6148
  9.7 5.3 %copy-start.16 = (f32[1,1,512]{2,1,0:T(1,128)}, f32[1,1,512]{2,1,0:T(1,128)S(1)}, u32[]{:S(2)}) copy-start(f32[1,1,512]{2,1,0:T(1,128)S(1)} %get-tuple-element.36) | copy-start | bytes 6148
  9.7 5.3 %copy-start.17 = (f32[1,1,512]{2,1,0:T(1,128)}, f32[1,1,512]{2,1,0:T(1,128)S(1)}, u32[]{:S(2)}) copy-start(f32[1,1,512]{2,1,0:T(1,128)S(1)} %get-tuple-element.37) | copy-start | bytes 6148
  9.7 25.6 %copy-start.29 = (s32[32]{0:T(128)S(1)}, s32[32]{0:T(128)}, u32[]{:S(2)}) copy-start(s32[32]{0:T(128)} %param.16) | copy-start | bytes 388
  15.1 23.3 %copy-start = (bf16[512,512]{1,0:T(8,128)(2,1)}, bf16[512,512]{1,0:T(8,128)(2,1)S(1)}, u32[]{:S(2)}) copy-start(bf16[512,512]{1,0:T(8,128)(2,1)S(1)} %multiply_convert_fusion) | copy-start | bytes 1572868
  15.1 22.2 %copy-start.3 = (bf16[512,512]{1,0:T(8,128)(2,1)S(1)}, bf16[512,512]{1,0:T(8,128)(2,1)}, u32[]{:S(2)}) copy-start(bf16[512,512]{1,0:T(8,128)(2,1)} %param.9) | copy-start | bytes 1572868
  17.1 21.9 %copy-start.27 = (bf16[4,32]{1,0:T(4,128)(2,1)S(1)}, bf16[4,32]{1,0:T(4,128)(2,1)}, u32[]{:S(2)}) copy-start(bf16[4,32]{1,0:T(4,128)(2,1)} %param.14) | copy-start | bytes 772
  18.1 113.7 %all-to-all-start = ((bf16[32,1,8,1536]{3,2,1,0:T(8,128)(2,1)}), bf16[32,1,8,1536]{3,2,1,0:T(8,128)(2,1)}, u32[]{:S(2)}, u32[]{:S(2)}) async-start(bf16[32,1,8,1536]{3,2,1,0:T(8,128)(2,1)} %stack.3), calls=%async_computation | async-start | bytes 1572864 | tf_op jit(solution)/shard_map/all_to_all | solution.py:11
  126.0 1.6 slice-start
  127.6 0.7 copy-start.30
  127.6 2.6 %copy-start.28 = (bf16[512]{0:T(512)(128)(2,1)S(1)}, bf16[512]{0:T(512)(128)(2,1)}, u32[]{:S(2)}) copy-start(bf16[512]{0:T(512)(128)(2,1)} %param.15) | copy-start | bytes 3076
  128.2 35.5 %slice-start.1 = ((bf16[512,512]{1,0:T(8,128)(2,1)}), bf16[504,512]{1,0:T(8,128)(2,1)S(1)}, s32[]{:S(2)}) async-start(bf16[512,512]{1,0:T(8,128)(2,1)} %copy-done), calls=%async_computation.3 | async-start | bytes 1032192 | tf_op jit(solution)/shard_map/slice | solution.py:101
  164.8 6.0 %copy-start.1 = (bf16[512,512]{1,0:T(8,128)(2,1)S(1)}, bf16[512,512]{1,0:T(8,128)(2,1)}, u32[]{:S(2)}) copy-start(bf16[512,512]{1,0:T(8,128)(2,1)} %get-tuple-element.9) | copy-start | bytes 1572868
  175.0 1.0 copy-start.2
  175.0 1.0 copy-start.18
  175.0 1.0 copy-start.19
  175.0 1.0 copy-start.20
  175.0 1.0 copy-start.21
  175.0 1.0 copy-start.22
  175.0 1.0 copy-start.23
  175.0 1.0 copy-start.24
  175.0 1.0 copy-start.26
  175.5 53.2 %copy-start.25 = (f32[512]{0:T(512)S(1)}, f32[512]{0:T(512)}, u32[]{:S(2)}) copy-start(f32[512]{0:T(512)} %convert_element_type.432) | copy-start | bytes 6148
Sparse Core Ops, SparseCore 0:
  15.9 146.8 all-gather.3
